TPU v7x, 256 devices: a whole 4x4x8 slice. The times are simulated.
256 devices in a mesh: row: 16 (over x, y_hi, core), col: 16 (over y_lo, z).
Axes of the slice: x: 4, y: 4 (y_hi: 2, y_lo: 2; y = y_hi * 2 + y_lo), z: 8, core: 2. Of those that a mesh axis runs over, the one named last changes fastest.
Arguments:
- pair: bfloat16 [2048, 64, 128], P('row', 'col'), may hold values from -6 to 6
- norm_gain: float32 [128], replicated, may hold values from 0.1 to 1.9
- norm_offset: float32 [128], replicated, may hold values from -3 to 3
- w_query: bfloat16 [128, 128], replicated, may hold values from -0.5 to 0.5
- w_key: bfloat16 [128, 128], replicated, may hold values from -0.5 to 0.5
- w_value: bfloat16 [128, 128], replicated, may hold values from -0.5 to 0.5
- w_gate: bfloat16 [128, 128], replicated, may hold values from -0.5 to 0.5
- gate_bias: float32 [128], replicated, may hold values from -4 to 4
- w_out: bfloat16 [128, 128], replicated, may hold values from -0.5 to 0.5
- out_bias: float32 [128], replicated, may hold values from -3 to 3
- bias: bfloat16 [4, 2048, 2048], P(None, 'row', 'col'), may hold values from -16 to 310
- chain_offset: float32 [4], replicated, may hold values from -3 to 1
- chain_ids: int32 [2048], replicated, may hold values from 0 to 7, never falling along the last dimension, each value on 1 to 512 neighbouring positions
- tile_mask: int32 [16, 16], replicated, may hold values from 0 to 1, as said below
Outputs:
- update: bfloat16 [2048, 64, 128], P('row', 'col')
Inputs may be any that keep to these rules, and one draw needn't show every extreme that they name: `tile_mask`: every tile on the diagonal is 1; each block row holds at most 8 ones, and the last block row holds exactly that many.
All inputs are finite; a program needn't handle non-finite values.
Results may differ from a plain program's by a relative error of at most 0.0047.
Values may be sent and summed in bfloat16 or wider, within the bound.
A program may use at most 128 MiB of HBM per device.

v0:
```python
import jax
import jax.numpy as jnp
from jax import lax
from jax.sharding import PartitionSpec as P

H = 4
DH = 32
TILE = 128
HD = 128


def layer_norm(pair, norm_gain, norm_offset):
    values = pair.astype(jnp.float32)
    center = values - jnp.mean(values, -1, keepdims=True)
    spread = jnp.mean(center * center, -1, keepdims=True)
    return (center * lax.rsqrt(spread + 1e-05) * norm_gain + norm_offset).astype(jnp.bfloat16)


def absorb(state, queries, key_piece, value_piece, bias_part, cross_part, allowed, chain_offset):
    running, totals, summed = state
    scores = jnp.einsum("ijhd,kjhd->jhik", queries, key_piece, preferred_element_type=jnp.float32)
    scores = (
        scores
        + bias_part.astype(jnp.float32)[None]
        + chain_offset[None, :, None, None] * cross_part[None, None]
    )
    scores = jnp.where(allowed[None, None], scores, -1e30)
    fresh = jnp.maximum(running, jnp.max(scores, -1))
    expo = jnp.where(allowed[None, None], jnp.exp(scores - fresh[..., None]), 0.0)
    totals = jnp.sum(expo, -1)
    summed = jnp.einsum(
        "jhik,kjhd->jhid",
        expo.astype(jnp.bfloat16),
        value_piece,
        preferred_element_type=jnp.float32,
    )
    return (fresh, totals, summed)


def on_device(
    pair,
    norm_gain,
    norm_offset,
    w_query,
    w_key,
    w_value,
    w_gate,
    gate_bias,
    w_out,
    out_bias,
    bias,
    chain_offset,
    chain_ids,
    tile_mask,
):
    rows, columns, channels = pair.shape
    blocks = tile_mask.shape[0]
    row_tiles = rows // TILE
    my_start = lax.axis_index("row") * rows
    mask_rows = lax.dynamic_slice_in_dim(tile_mask, lax.axis_index("row") * row_tiles, row_tiles, 0)
    block_ids = jnp.arange(blocks, dtype=jnp.int32)
    bias_rows = lax.all_gather(bias, "col", axis=2, tiled=True)
    normed = layer_norm(pair, norm_gain, norm_offset)
    flat = normed.reshape(rows * columns, channels)
    scale = 1.0 / DH**0.5
    queries = (
        (jnp.dot(flat, w_query, preferred_element_type=jnp.float32) * scale)
        .astype(jnp.bfloat16)
        .reshape(rows, columns, H, DH)
    )
    gate = jax.nn.sigmoid(jnp.dot(flat, w_gate, preferred_element_type=jnp.float32) + gate_bias)
    w_both = jnp.concatenate([w_key, w_value], axis=1)
    chain_rows = lax.dynamic_slice_in_dim(chain_ids, my_start, rows)
    initial = (
        jnp.full((columns, H, rows), -1e30, jnp.float32),
        jnp.zeros((columns, H, rows), jnp.float32),
        jnp.zeros((columns, H, rows, DH), jnp.float32),
    )
    both = (
        jnp.dot(flat, w_both, preferred_element_type=jnp.float32)
        .astype(jnp.bfloat16)
        .reshape(rows, columns, 2 * HD)
    )
    key_local = both[:, :, :HD]
    value_local = both[:, :, HD:]
    pieces = (
        lax.all_gather(key_local, "row", axis=0, tiled=True),
        lax.all_gather(value_local, "row", axis=0, tiled=True),
    )
    count = pieces[0].shape[0]
    key_piece = pieces[0].reshape(count, columns, H, DH)
    value_piece = pieces[1].reshape(count, columns, H, DH)
    count = key_piece.shape[0]
    cross_part = (chain_rows[:, None] != chain_ids[None, :]).astype(jnp.float32)
    key_blocks = jnp.arange(count, dtype=jnp.int32) // TILE
    onehot = (key_blocks[None, :] == block_ids[:, None]).astype(jnp.int32)
    tile_allowed = jnp.dot(mask_rows, onehot)
    allowed = jnp.repeat(tile_allowed, TILE, axis=0) > 0
    final = absorb(
        initial, queries, key_piece, value_piece, bias_rows, cross_part, allowed, chain_offset
    )
    attended = final[2] / final[1][..., None]
    attended = jnp.transpose(attended, (2, 0, 1, 3)).reshape(rows * columns, HD)
    gated = (gate * attended).astype(jnp.bfloat16)
    update = jnp.dot(gated, w_out, preferred_element_type=jnp.float32) + out_bias
    return update.astype(jnp.bfloat16).reshape(rows, columns, channels)


def solution(mesh):
    placed = (
        P("row", "col", None),
        P(),
        P(),
        P(),
        P(),
        P(),
        P(),
        P(),
        P(),
        P(),
        P(None, "row", "col"),
        P(),
        P(),
        P(),
    )
    return jax.shard_map(
        on_device, mesh=mesh, in_specs=placed, out_specs=P("row", "col", None), check_vma=False
    )
```

profile of v0, /device:TPU:1, one launch (start us, length us, event | category | flops | bytes accessed | tf_op | source)
XLA Modules:
  0.0 220.6 jit_solution(17884730410167850007)
XLA Ops:
  6.5 1.1 convert_reduce_fusion
  7.7 1.3 fusion.24
  9.0 1.3 fusion.27
  10.3 1.0 convolution_convert_fusion
  11.3 0.8 fusion.43
  12.2 0.7 all-gather.6.cloned.1.call-update
  12.9 0.7 all-gather.8.cloned.1.call-update
  13.8 0.9 fusion.30
  15.0 0.8 dynamic_slice.7
  15.7 0.8 compare_convert_fusion
  16.6 3.2 %broadcast_multiply_fusion = f32[4,128,2048]{2,1,0:T(8,128)} fusion(f32[128,2048]{1,0:T(8,128)S(1)} %compare_convert_fusion, f32[4]{0:T(128)} %param.25), kind=kLoop, calls=%fused_computation.7 | loop fusion | flops 1048576 | bytes 5242896 | tf_op jit(solution)/shard_map/mul | solution.py:25
  19.7 50.3 %all-gather.4.cloned.1.call-done = bf16[2048,4,128]{2,1,0:T(4,128)(2,1)} async-done(((bf16[128,4,128]{2,1,0:T(4,128)(2,1)}), bf16[2048,4,128]{2,1,0:T(4,128)(2,1)}) %all-gather.4.cloned.1.call-update) | async-done | bytes 2097168 | tf_op jit(solution)/shard_map/all_gather | solution.py:87
  70.0 4.4 %copy.22 = bf16[2048,4,128]{0,2,1:T(8,128)(2,1)} copy(bf16[2048,4,128]{2,1,0:T(4,128)(2,1)} %all-gather.4.cloned.1.call-done) | data formatting | bytes 4194304 | tf_op jit(solution)/shard_map/all_gather | solution.py:87
  74.3 58.2 %all-gather.6.cloned.1.call-done = bf16[4,128,2048]{2,1,0:T(8,128)(2,1)} async-done(((bf16[4,128,128]{2,1,0:T(8,128)(2,1)}), bf16[4,128,2048]{2,1,0:T(8,128)(2,1)}) %all-gather.6.cloned.1.call-update) | async-done | bytes 2097168 | tf_op jit(solution)/shard_map/all_gather | solution.py:62
  132.5 4.1 %convert_element_type.36 = f32[4,128,2048]{2,1,0:T(8,128)} convert(bf16[4,128,2048]{2,1,0:T(8,128)(2,1)} %all-gather.6.cloned.1.call-done) | non-fusion elementwise | flops 1048576 | bytes 6291456 | tf_op jit(solution)/shard_map/convert_element_type | solution.py:24
  136.6 5.6 %fusion = (f32[4,4,128]{2,1,0:T(4,128)S(1)}, f32[4,4,128,2048]{3,2,1,0:T(8,128)S(1)}) fusion(f32[4,128,2048]{2,1,0:T(8,128)} %broadcast_multiply_fusion, f32[4,128,2048]{2,1,0:T(8,128)} %convert_element_type.36, pred[2048]{0:T(1024)(128)(4,1)S(1)} %broadcast_compare_fusion, bf16[2048,4,4,32]{0,3,2,1:T(8,128)(2,1)} %bitcast.22, ...), kind=kOutput, calls=%fused_computation.2 | convolution fusion | flops 285210624 | bytes 27404288 | tf_op jit(solution)/shard_map/ijhd,kjhd->jhik/dot_general | solution.py:21
  142.3 5.7 %copy-done.1 = f32[4,4,128,2048]{3,2,1,0:T(8,128)} copy-done((f32[4,4,128,2048]{3,2,1,0:T(8,128)}, f32[4,4,128,2048]{3,2,1,0:T(8,128)S(1)}, u32[]{:S(2)}) %copy-start.1) | copy-done | bytes 16777240
  148.0 6.9 %fusion.1 = f32[4,4,128]{2,1,0:T(4,128)S(1)} fusion(f32[4,4,128,2048]{3,2,1,0:T(8,128)S(1)} %get-tuple-element.8, f32[4,4,128]{2,1,0:T(4,128)S(1)} %broadcast_maximum_fusion, f32[4,128,2048]{2,1,0:T(8,128)} %broadcast_multiply_fusion, f32[4,128,2048]{2,1,0:T(8,128)} %convert_element_type.36, pred[2048]{0:T(1024)(128)(4,1)S(1)} %broadcast_compare_fusion), kind=kLoop, calls=%fused_computation.3 | loop fusion | flops 25163776 | bytes 25184256 | tf_op jit(solution)/shard_map/reduce_sum | solution.py:30
  154.9 43.8 %all-gather.8.cloned.1.call-done = bf16[2048,4,128]{2,1,0:T(4,128)(2,1)} async-done(((bf16[128,4,128]{2,1,0:T(4,128)(2,1)}), bf16[2048,4,128]{2,1,0:T(4,128)(2,1)}) %all-gather.8.cloned.1.call-update) | async-done | bytes 2097168 | tf_op jit(solution)/shard_map/all_gather | solution.py:88
  198.7 3.0 %copy.24 = bf16[2048,4,128]{0,2,1:T(8,128)(2,1)S(1)} copy(bf16[2048,4,128]{2,1,0:T(4,128)(2,1)} %all-gather.8.cloned.1.call-done) | data formatting | bytes 4194304 | tf_op jit(solution)/shard_map/all_gather | solution.py:88
  201.7 10.3 %fusion.17 = f32[128,4,4,32]{0,3,2,1:T(8,128)S(1)} fusion(bf16[2048,4,4,32]{0,3,2,1:T(8,128)(2,1)S(1)} %bitcast.23, f32[4,4,128,2048]{3,2,1,0:T(8,128)} %copy-done.1, f32[4,4,128]{2,1,0:T(4,128)S(1)} %broadcast_maximum_fusion, f32[4,128,2048]{2,1,0:T(8,128)} %broadcast_multiply_fusion, f32[4,128,2048]{2,1,0:T(8,128)} %convert_element_type.36, ...), kind=kOutput, calls=%fused_computation.21 | convolution fusion | flops 293666816 | bytes 27543552 | tf_op jit(solution)/shard_map/jhik,kjhd->jhid/dot_general | solution.py:31
  212.0 0.6 copy.25
  212.6 0.5 reshape.106
  213.1 1.0 fusion.16
  (23 shorter events, 0.6 us)
Async XLA Ops:
  6.5 7.1 %copy-start = (bf16[128,128]{1,0:T(8,128)(2,1)S(1)}, bf16[128,128]{1,0:T(8,128)(2,1)}, u32[]{:S(2)}) copy-start(bf16[128,128]{1,0:T(8,128)(2,1)} %param.17) | copy-start | bytes 98308
  6.5 63.4 %all-gather.4.cloned.1.call-start = ((), (), s32[]{:S(2)}) async-start(), calls=%async_computation | async-start | bytes 2228224 | tf_op jit(solution)/shard_map/all_gather | solution.py:87
  12.1 120.4 %all-gather.6.cloned.1.call-start = ((), (), s32[]{:S(2)}) async-start(), calls=%async_computation.1 | async-start | bytes 2228224 | tf_op jit(solution)/shard_map/all_gather | solution.py:62
  12.9 185.8 %all-gather.8.cloned.1.call-start = ((), (), s32[]{:S(2)}) async-start(), calls=%async_computation.2 | async-start | bytes 2228224 | tf_op jit(solution)/shard_map/all_gather | solution.py:88
  142.2 5.7 %copy-start.1 = (f32[4,4,128,2048]{3,2,1,0:T(8,128)}, f32[4,4,128,2048]{3,2,1,0:T(8,128)S(1)}, u32[]{:S(2)}) copy-start(f32[4,4,128,2048]{3,2,1,0:T(8,128)S(1)} %get-tuple-element.8) | copy-start | bytes 50331652
  201.7 11.4 %copy-start.2 = (bf16[128,128]{1,0:T(8,128)(2,1)S(1)}, bf16[128,128]{1,0:T(8,128)(2,1)}, u32[]{:S(2)}) copy-start(bf16[128,128]{1,0:T(8,128)(2,1)} %param.22) | copy-start | bytes 98308
  201.7 11.4 %copy-start.3 = (bf16[128,128]{1,0:T(8,128)(2,1)S(1)}, bf16[128,128]{1,0:T(8,128)(2,1)}, u32[]{:S(2)}) copy-start(bf16[128,128]{1,0:T(8,128)(2,1)} %param.20) | copy-start | bytes 98308
  201.7 11.4 %copy-start.4 = (f32[128]{0:T(128)S(1)}, f32[128]{0:T(128)}, u32[]{:S(2)}) copy-start(f32[128]{0:T(128)} %param.23) | copy-start | bytes 1540
  201.7 11.4 %copy-start.5 = (f32[128]{0:T(128)S(1)}, f32[128]{0:T(128)}, u32[]{:S(2)}) copy-start(f32[128]{0:T(128)} %param.21) | copy-start | bytes 1540
Sparse Core Ops, SparseCore 0:
  12.2 57.6 all-gather.3
  71.7 60.7 all-gather.5
  135.2 63.4 all-gather.7
where the time goes:
time: 221 us
  waiting for transfers between devices  154 us (70%)
  matrix products  18.9 us (9%)
  other arithmetic  18.7 us (8%)
  local copies, waits for them, and re-layouts  16 us (7%)
  between operations  13.3 us (6%)
    all_gather x1, waiting for transfers between devices, on_device(): bias_rows = lax.all_gather(bias, 'col', axis=2, tiled=True)  58.2 us
    all_gather x1, waiting for transfers between devices, on_device(): lax.all_gather(key_local, 'row', axis=0, tiled=True)  50.3 us
    all_gather x1, waiting for transfers between devices, on_device(): lax.all_gather(value_local, 'row', axis=0, tiled=True)  43.8 us
    dot_general x1, matrix products, absorb(): jnp.einsum('jhik,kjhd->jhid', expo.astype(jnp.bfloat16), value_piece, pre...  10.3 us
    reduce_sum x1, other arithmetic, absorb(): totals = jnp.sum(expo, -1)  6.95 us
    unnamed x12, local copies, waits for them, and re-layouts  5.73 us
    dot_general x1, matrix products, absorb(): jnp.einsum('ijhd,kjhd->jhik', queries, key_piece, preferred_element_type=...  5.63 us
  transfers between devices with their start and end apart: 3, of which 3 were waited for; matrix products, arithmetic and copies ran while one was open for 12% of the time, Pallas kernels for 0%

commit v1 on v0

v1 whole, which is shorter than its diff:
```python
import functools
import math

import jax
import jax.numpy as jnp
from jax import lax
from jax.experimental import pallas as pl
from jax.experimental.pallas import tpu as pltpu
from jax.sharding import PartitionSpec as P

H = 4
DH = 32
TILE = 128
HD = 128
COLS = 4
NB = 16
NSEL = 8
HALF = 256
LOG2E = math.log2(math.e)
MESH = pl.DeviceIdType.MESH
F32 = jnp.float32
BF16 = jnp.bfloat16

BIAS_IDS = ["A+1", "A-1", "A+2", "A-2", "A+3", "A-3", "A4", "B0", "B+1", "B-1", "B+2", "B-2", "B+3", "B-3", "B4"]
NORM_IDS = ["P+1", "P-1", "P2", "Q0", "Q+1", "Q-1", "Q2"]
SIB_IDS = ["P0"] + NORM_IDS


def nt(a, b):
    return lax.dot_general(a, b, (((1,), (1,)), ((), ())), preferred_element_type=F32)


def nn(a, b):
    return jnp.dot(a, b, preferred_element_type=F32)


def kernel(
    mask_ref,
    offset_ref,
    pair_ref,
    gain_ref,
    shift_ref,
    wq_ref,
    wk_ref,
    wv_ref,
    wg_ref,
    gb_ref,
    wo_ref,
    ob_ref,
    bias_ref,
    chain_ref,
    out_ref,
    bias_all,
    norm_all,
    rows_f32,
    qp_ref,
    gate_ref,
    bx_ref,
    s_ref,
    bias_send,
    bias_recv,
    norm_send,
    norm_recv,
    sib_send,
    sib_recv,
    local_sem,
):
    r = lax.axis_index("row")
    c = lax.axis_index("col")
    core, yh, x = r % 2, (r // 2) % 2, r // 4
    z, yl = c % 8, c // 8

    def row_of(dx, flip):
        return ((x + dx + 4) % 4) * 4 + ((yh + flip) % 2) * 2 + core

    def col_of(dz, flip):
        return ((yl + flip) % 2) * 8 + (z + dz + 8) % 8

    up = (r, col_of(1, 0))
    down = (r, col_of(-1, 0))
    across = (r, col_of(0, 1))
    right = (row_of(1, 0), c)
    left = (row_of(-1, 0), c)
    far = (row_of(0, 1), c)
    sib_row = r + 1 - 2 * core
    sib = (sib_row, c)

    barrier = pltpu.get_barrier_semaphore()
    for peer in (up, down, across, right, left, far, sib):
        pl.semaphore_signal(barrier, inc=1, device_id=peer, device_id_type=MESH)

    values = pair_ref[...].astype(F32)
    center = values - jnp.mean(values, -1, keepdims=True)
    spread = jnp.mean(center * center, -1, keepdims=True)
    rows_f32[...] = center * lax.rsqrt(spread + 1e-05) * gain_ref[...] + shift_ref[...]
    for j in range(COLS):
        norm_all[r, j // 2, (j % 2) * TILE:(j % 2 + 1) * TILE, :] = rows_f32[
            pl.ds(j, TILE, stride=COLS), :
        ].astype(BF16)

    pl.semaphore_wait(barrier, 7)

    sends = []

    def bias_slot(name):
        flip = 0 if name[0] == "A" else 1
        dist = int(name[1:])
        return col_of(-dist, flip)

    def norm_slot(name, base=None):
        flip = 0 if name[0] == "P" else 1
        dist = int(name[1:])
        return row_of(-dist, flip)

    def send_bias(src_name, p, peer, as_name):
        if src_name == "A0":
            src = bias_ref.at[p]
        else:
            src = bias_all.at[bias_slot(src_name), p]
        copy = pltpu.make_async_remote_copy(
            src_ref=src,
            dst_ref=bias_all.at[bias_slot(src_name), p],
            send_sem=bias_send.at[len([s for s in sends if s[0] == "b"])],
            recv_sem=bias_recv.at[BIAS_IDS.index(as_name) * 2 + p],
            device_id=peer,
            device_id_type=MESH,
        )
        copy.start()
        sends.append(("b", copy))

    def wait_bias(name, p):
        ref = bias_all.at[bias_slot(name), p]
        sem = bias_recv.at[BIAS_IDS.index(name) * 2 + p]
        pltpu.make_async_remote_copy(
            src_ref=ref, dst_ref=ref, send_sem=bias_send.at[0], recv_sem=sem, device_id=up, device_id_type=MESH
        ).wait_recv()

    def send_norm(src_name, p, peer, as_name):
        slot = norm_slot(src_name)
        copy = pltpu.make_async_remote_copy(
            src_ref=norm_all.at[slot, p],
            dst_ref=norm_all.at[slot, p],
            send_sem=norm_send.at[len([s for s in sends if s[0] == "n"])],
            recv_sem=norm_recv.at[NORM_IDS.index(as_name) * 2 + p],
            device_id=peer,
            device_id_type=MESH,
        )
        copy.start()
        sends.append(("n", copy))

    def wait_norm(name, p):
        ref = norm_all.at[norm_slot(name), p]
        sem = norm_recv.at[NORM_IDS.index(name) * 2 + p]
        pltpu.make_async_remote_copy(
            src_ref=ref, dst_ref=ref, send_sem=norm_send.at[0], recv_sem=sem, device_id=up, device_id_type=MESH
        ).wait_recv()

    def send_sib(name):
        slot = norm_slot(name)
        copy = pltpu.make_async_remote_copy(
            src_ref=norm_all.at[slot],
            dst_ref=norm_all.at[slot],
            send_sem=sib_send.at[SIB_IDS.index(name)],
            recv_sem=sib_recv.at[SIB_IDS.index(name)],
            device_id=sib,
            device_id_type=MESH,
        )
        copy.start()
        sends.append(("s", copy))

    def wait_sib(name):
        ref = norm_all.at[norm_slot(name) + 1 - 2 * core]
        index = SIB_IDS.index(name)
        pltpu.make_async_remote_copy(
            src_ref=ref,
            dst_ref=ref,
            send_sem=sib_send.at[index],
            recv_sem=sib_recv.at[index],
            device_id=sib,
            device_id_type=MESH,
        ).wait_recv()

    for p in range(2):
        send_bias("A0", p, up, "A+1")
        send_bias("A0", p, down, "A-1")
        send_bias("A0", p, across, "B0")
        send_norm("P0", p, right, "P+1")
        send_norm("P0", p, left, "P-1")
        send_norm("P0", p, far, "Q0")
    send_sib("P0")
    own = pltpu.make_async_copy(bias_ref, bias_all.at[c], local_sem)
    own.start()

    mine = norm_all[r].reshape(COLS * TILE, HD)
    query = (nn(mine, wq_ref[...]) * (1.0 / DH**0.5)).astype(BF16)
    gate_ref[...] = jax.nn.sigmoid(nn(mine, wg_ref[...]) + gb_ref[...])
    head = lax.broadcasted_iota(jnp.int32, (TILE, HD), 1) // DH
    for j in range(COLS):
        part = query[j * TILE:(j + 1) * TILE]
        stacked = jnp.concatenate([jnp.where(head == h, part, jnp.zeros_like(part)) for h in range(H)], axis=0)
        qp_ref[j] = (nt(stacked, wk_ref[...]) * LOG2E).astype(BF16)

    picks = [jnp.int32(0) for _ in range(NSEL)]
    count = jnp.int32(0)
    for k in range(NB):
        flag = mask_ref[r, k]
        for n in range(NSEL):
            picks[n] = jnp.where((flag == 1) & (count == n), k, picks[n])
        count = count + jnp.where(flag == 1, 1, 0)
    pads = [jnp.where(n < count, 0.0, -1e30).astype(F32) for n in range(NSEL)]

    for p in range(2):
        wait_bias("A+1", p)
        send_bias("A+1", p, up, "A+2")
        wait_bias("A-1", p)
        send_bias("A-1", p, down, "A-2")
        wait_bias("B0", p)
        send_bias("B0", p, up, "B+1")
        send_bias("B0", p, down, "B-1")
        wait_norm("P+1", p)
        if p == 0:
            send_norm("P+1", p, right, "P2")
        wait_norm("P-1", p)
        if p == 1:
            send_norm("P-1", p, left, "P2")
        wait_norm("Q0", p)
        send_norm("Q0", p, right, "Q+1")
        send_norm("Q0", p, left, "Q-1")
    for name in ("P+1", "P-1", "Q0"):
        send_sib(name)
    for p in range(2):
        wait_bias("A+2", p)
        send_bias("A+2", p, up, "A+3")
        send_bias("A+2", p, across, "B+2")
        wait_bias("A-2", p)
        send_bias("A-2", p, down, "A-3")
        send_bias("A-2", p, across, "B-2")
    for p in range(2):
        wait_norm("Q+1", p)
        if p == 0:
            send_norm("Q+1", p, right, "Q2")
        wait_norm("Q-1", p)
        if p == 1:
            send_norm("Q-1", p, left, "Q2")
    wait_norm("P2", 0)
    wait_norm("P2", 1)
    for name in ("P2", "Q+1", "Q-1"):
        send_sib(name)
    for p in range(2):
        wait_bias("B+2", p)
        send_bias("B+2", p, up, "B+3")
        wait_bias("B-2", p)
        send_bias("B-2", p, down, "B-3")
        wait_bias("A+3", p)
        if p == 0:
            send_bias("A+3", p, up, "A4")
        wait_bias("A-3", p)
        if p == 1:
            send_bias("A-3", p, down, "A4")
    wait_norm("Q2", 0)
    wait_norm("Q2", 1)
    send_sib("Q2")
    for p in range(2):
        wait_bias("A4", p)
        send_bias("A4", p, across, "B4")
    for name in ("B+1", "B-1", "B+3", "B-3", "B4"):
        for p in range(2):
            wait_bias(name, p)
    for name in SIB_IDS:
        wait_sib(name)
    own.wait()

    chain_i = jnp.transpose(jnp.broadcast_to(chain_ref[pl.ds(r, 1), :], (TILE, TILE)))
    for n in range(NSEL):
        chain_k = chain_ref[pl.ds(picks[n], 1), :]
        differs = chain_i != chain_k
        for h in range(H):
            part = bias_all[picks[n], h // 2, (h % 2) * TILE:(h % 2 + 1) * TILE, :].astype(F32)
            total = part + jnp.where(differs, offset_ref[h], 0.0) + pads[n]
            bx_ref[n // 2, h * TILE:(h + 1) * TILE, (n % 2) * TILE:(n % 2 + 1) * TILE] = total * LOG2E

    for j in range(COLS):
        keys = [
            jnp.concatenate(
                [
                    norm_all[picks[2 * m + e], j // 2, (j % 2) * TILE:(j % 2 + 1) * TILE, :]
                    for e in range(2)
                ],
                axis=0,
            )
            for m in range(NSEL // 2)
        ]
        queries = qp_ref[j]
        peak = None
        for m in range(NSEL // 2):
            scores = nt(queries, keys[m]) + bx_ref[m]
            s_ref[m] = scores
            best = jnp.maximum(scores[:, :TILE], scores[:, TILE:])
            peak = best if peak is None else jnp.maximum(peak, best)
        peak = jnp.max(peak, axis=-1, keepdims=True)
        total, summed = None, None
        for m in range(NSEL // 2):
            expo = jnp.exp2(s_ref[m] - peak)
            part = expo[:, :TILE] + expo[:, TILE:]
            total = part if total is None else total + part
            prod = nn(expo.astype(BF16), keys[m])
            summed = prod if summed is None else summed + prod
        total = jnp.sum(total, axis=-1, keepdims=True)
        mixed = summed / total
        high = mixed.astype(BF16)
        low = (mixed - high.astype(F32)).astype(BF16)
        heads = nn(high, wv_ref[...]) + nn(low, wv_ref[...])
        attended = jnp.where(head == 0, heads[:TILE], 0.0)
        for h in range(1, H):
            attended = jnp.where(head == h, heads[h * TILE:(h + 1) * TILE], attended)
        gated = (gate_ref[j * TILE:(j + 1) * TILE, :] * attended).astype(BF16)
        rows_f32[pl.ds(j, TILE, stride=COLS), :] = nn(gated, wo_ref[...]) + ob_ref[...]
    out_ref[...] = rows_f32[...].astype(BF16)

    for _, copy in sends:
        copy.wait_send()


def on_device(
    pair,
    norm_gain,
    norm_offset,
    w_query,
    w_key,
    w_value,
    w_gate,
    gate_bias,
    w_out,
    out_bias,
    bias,
    chain_offset,
    chain_ids,
    tile_mask,
):
    smem = pl.BlockSpec(memory_space=pltpu.SMEM)
    vmem = pl.BlockSpec(memory_space=pltpu.VMEM)
    hbm = pl.BlockSpec(memory_space=pl.ANY)
    out = pl.pallas_call(
        kernel,
        out_shape=jax.ShapeDtypeStruct((TILE * COLS, HD), BF16),
        in_specs=[smem, smem] + [vmem] * 10 + [hbm, vmem],
        out_specs=vmem,
        scratch_shapes=[
            pltpu.VMEM((NB, 2, HALF, TILE), BF16),
            pltpu.VMEM((NB, 2, HALF, HD), BF16),
            pltpu.VMEM((TILE * COLS, HD), F32),
            pltpu.VMEM((COLS, H * TILE, HD), BF16),
            pltpu.VMEM((COLS * TILE, HD), F32),
            pltpu.VMEM((NSEL // 2, H * TILE, 2 * TILE), F32),
            pltpu.VMEM((NSEL // 2, H * TILE, 2 * TILE), F32),
            pltpu.SemaphoreType.DMA((32,)),
            pltpu.SemaphoreType.DMA((30,)),
            pltpu.SemaphoreType.DMA((14,)),
            pltpu.SemaphoreType.DMA((14,)),
            pltpu.SemaphoreType.DMA((8,)),
            pltpu.SemaphoreType.DMA((8,)),
            pltpu.SemaphoreType.DMA,
        ],
        compiler_params=pltpu.CompilerParams(
            collective_id=0, has_side_effects=True, vmem_limit_bytes=48 * 1024 * 1024
        ),
        cost_estimate=pl.CostEstimate(flops=1 << 30, bytes_accessed=1 << 20, transcendentals=1 << 21),
    )(
        tile_mask,
        chain_offset,
        pair.reshape(TILE * COLS, HD),
        norm_gain.reshape(1, HD),
        norm_offset.reshape(1, HD),
        w_query,
        w_key,
        w_value,
        w_gate,
        gate_bias.reshape(1, HD),
        w_out,
        out_bias.reshape(1, HD),
        bias.reshape(2, HALF, TILE),
        chain_ids.reshape(NB, TILE),
    )
    return out.reshape(TILE, COLS, HD)


def solution(mesh):
    placed = (
        P("row", "col", None),
        P(),
        P(),
        P(),
        P(),
        P(),
        P(),
        P(),
        P(),
        P(),
        P(None, "row", "col"),
        P(),
        P(),
        P(),
    )
    return jax.shard_map(
        on_device, mesh=mesh, in_specs=placed, out_specs=P("row", "col", None), check_vma=False
    )
```

time: 221 us -> 45.8 us (0.21)
  the two profiles are of different devices: /device:TPU:1 before, /device:TPU:2 now
where the time goes in v1:
time: 45.8 us; the launch traced here: 45.2 us
  Pallas kernels  37.5 us (82%)
  local copies, waits for them, and re-layouts  7.65 us (17%)
    pallas_call x1, Pallas kernels, on_device(): pl.pallas_call(kernel, out_shape=jax.ShapeDtypeStruct((TILE * COLS, HD),...  37.5 us
    unnamed x29, local copies, waits for them, and re-layouts  7.65 us

profile of v1, /device:TPU:2, one launch (start us, length us, event | category | flops | bytes accessed | tf_op | source)
XLA Modules:
  0.0 45.2 jit_solution(8211222620369668041)
XLA Ops:
  0.0 0.0 copy-start.7
  0.0 0.0 copy-start.12
  0.0 0.0 copy-start.13
  0.0 0.0 copy-start.9
  0.0 0.0 copy-start.10
  0.0 0.0 copy-start.11
  0.0 0.7 %copy-done.7 = s32[16,16]{1,0:T(8,128)S(1)} copy-done((s32[16,16]{1,0:T(8,128)S(1)}, s32[16,16]{1,0:T(8,128)}, u32[]{:S(2)}) %copy-start.7) | copy-done | bytes 1048
  0.7 0.0 copy-done.12
  0.7 0.0 copy-done.13
  0.7 0.0 copy-done.9
  0.7 0.0 copy-done.10
  0.7 0.0 copy-done.11
  0.7 0.0 copy-start
  0.7 0.9 %copy-done = bf16[128,4,128]{2,1,0:T(4,128)(2,1)S(1)} copy-done((bf16[128,4,128]{2,1,0:T(4,128)(2,1)S(1)}, bf16[128,4,128]{2,1,0:T(4,128)(2,1)}, u32[]{:S(2)}) %copy-start) | copy-done | bytes 131096
  1.6 0.0 copy-start.1
  1.6 0.9 %copy-done.1 = bf16[4,128,128]{2,1,0:T(8,128)(2,1)S(1)} copy-done((bf16[4,128,128]{2,1,0:T(8,128)(2,1)S(1)}, bf16[4,128,128]{2,1,0:T(8,128)(2,1)}, u32[]{:S(2)}) %copy-start.1) | copy-done | bytes 131096
  2.5 0.8 %copy-done.2 = bf16[128,128]{1,0:T(8,128)(2,1)S(1)} copy-done((bf16[128,128]{1,0:T(8,128)(2,1)S(1)}, bf16[128,128]{1,0:T(8,128)(2,1)}, u32[]{:S(2)}) %copy-start.2) | copy-done | bytes 32792
  3.3 0.8 %copy-done.3 = bf16[128,128]{1,0:T(8,128)(2,1)S(1)} copy-done((bf16[128,128]{1,0:T(8,128)(2,1)S(1)}, bf16[128,128]{1,0:T(8,128)(2,1)}, u32[]{:S(2)}) %copy-start.3) | copy-done | bytes 32792
  4.1 0.8 %copy-done.4 = bf16[128,128]{1,0:T(8,128)(2,1)S(1)} copy-done((bf16[128,128]{1,0:T(8,128)(2,1)S(1)}, bf16[128,128]{1,0:T(8,128)(2,1)}, u32[]{:S(2)}) %copy-start.4) | copy-done | bytes 32792
  4.8 0.8 %copy-done.5 = bf16[128,128]{1,0:T(8,128)(2,1)S(1)} copy-done((bf16[128,128]{1,0:T(8,128)(2,1)S(1)}, bf16[128,128]{1,0:T(8,128)(2,1)}, u32[]{:S(2)}) %copy-start.5) | copy-done | bytes 32792
  5.6 0.8 %copy-done.6 = bf16[128,128]{1,0:T(8,128)(2,1)S(1)} copy-done((bf16[128,128]{1,0:T(8,128)(2,1)S(1)}, bf16[128,128]{1,0:T(8,128)(2,1)}, u32[]{:S(2)}) %copy-start.6) | copy-done | bytes 32792
  6.3 0.7 %copy-done.8 = s32[2048]{0:T(1024)S(1)} copy-done((s32[2048]{0:T(1024)S(1)}, s32[2048]{0:T(1024)}, u32[]{:S(2)}) %copy-start.8) | copy-done | bytes 8216
  7.0 37.5 %shard_map.136 = bf16[512,128]{1,0:T(8,128)(2,1)S(1)} custom-call(s32[16,16]{1,0:T(8,128)S(1)} %copy-done.7, f32[4]{0:T(128)S(1)} %copy-done.9, bf16[512,128]{1,0:T(8,128)(2,1)S(1)} %bitcast.9, f32[1,128]{1,0:T(1,128)S(1)} %bitcast.12, f32[1,128]{1,0:T(1,128)S(1)} %bitcast.13, bf16[128,128]{1,0:T(8,128)(2,1)S(1)} %copy-done.2, ...), custom_call_target="tpu_custom_call" | custom-call | flops 1073741824 | bytes 1048576 | tf_op jit(solution)/shard_map/pallas_call | solution.py:343
  44.6 0.7 %copy.16 = bf16[128,4,128]{2,1,0:T(4,128)(2,1)} copy(bf16[128,4,128]{2,1,0:T(4,128)(2,1)S(1)} %bitcast.8) | data formatting | bytes 262144
  (6 shorter events, 0.0 us)
Async XLA Ops:
  0.0 0.7 %copy-start.7 = (s32[16,16]{1,0:T(8,128)S(1)}, s32[16,16]{1,0:T(8,128)}, u32[]{:S(2)}) copy-start(s32[16,16]{1,0:T(8,128)} %mask_ref.1) | copy-start | bytes 3076
  0.0 0.7 %copy-start.12 = (f32[128]{0:T(128)S(1)}, f32[128]{0:T(128)}, u32[]{:S(2)}) copy-start(f32[128]{0:T(128)} %param.21) | copy-start | bytes 1540
  0.0 0.7 %copy-start.13 = (f32[128]{0:T(128)S(1)}, f32[128]{0:T(128)}, u32[]{:S(2)}) copy-start(f32[128]{0:T(128)} %param.23) | copy-start | bytes 1540
  0.0 0.7 %copy-start.9 = (f32[4]{0:T(128)S(1)}, f32[4]{0:T(128)}, u32[]{:S(2)}) copy-start(f32[4]{0:T(128)} %offset_ref.1) | copy-start | bytes 52
  0.0 0.7 %copy-start.10 = (f32[128]{0:T(128)S(1)}, f32[128]{0:T(128)}, u32[]{:S(2)}) copy-start(f32[128]{0:T(128)} %param.15) | copy-start | bytes 1540
  0.0 0.7 %copy-start.11 = (f32[128]{0:T(128)S(1)}, f32[128]{0:T(128)}, u32[]{:S(2)}) copy-start(f32[128]{0:T(128)} %param.16) | copy-start | bytes 1540
  0.7 0.9 %copy-start = (bf16[128,4,128]{2,1,0:T(4,128)(2,1)S(1)}, bf16[128,4,128]{2,1,0:T(4,128)(2,1)}, u32[]{:S(2)}) copy-start(bf16[128,4,128]{2,1,0:T(4,128)(2,1)} %param.14) | copy-start | bytes 393220
  1.6 0.9 %copy-start.1 = (bf16[4,128,128]{2,1,0:T(8,128)(2,1)S(1)}, bf16[4,128,128]{2,1,0:T(8,128)(2,1)}, u32[]{:S(2)}) copy-start(bf16[4,128,128]{2,1,0:T(8,128)(2,1)} %param.24) | copy-start | bytes 393220
  2.5 0.8 %copy-start.2 = (bf16[128,128]{1,0:T(8,128)(2,1)S(1)}, bf16[128,128]{1,0:T(8,128)(2,1)}, u32[]{:S(2)}) copy-start(bf16[128,128]{1,0:T(8,128)(2,1)} %wq_ref.1) | copy-start | bytes 98308
  3.3 0.8 %copy-start.3 = (bf16[128,128]{1,0:T(8,128)(2,1)S(1)}, bf16[128,128]{1,0:T(8,128)(2,1)}, u32[]{:S(2)}) copy-start(bf16[128,128]{1,0:T(8,128)(2,1)} %wk_ref.1) | copy-start | bytes 98308
  4.1 0.8 %copy-start.4 = (bf16[128,128]{1,0:T(8,128)(2,1)S(1)}, bf16[128,128]{1,0:T(8,128)(2,1)}, u32[]{:S(2)}) copy-start(bf16[128,128]{1,0:T(8,128)(2,1)} %wv_ref.1) | copy-start | bytes 98308
  4.8 0.8 %copy-start.5 = (bf16[128,128]{1,0:T(8,128)(2,1)S(1)}, bf16[128,128]{1,0:T(8,128)(2,1)}, u32[]{:S(2)}) copy-start(bf16[128,128]{1,0:T(8,128)(2,1)} %wg_ref.1) | copy-start | bytes 98308
  5.6 0.8 %copy-start.6 = (bf16[128,128]{1,0:T(8,128)(2,1)S(1)}, bf16[128,128]{1,0:T(8,128)(2,1)}, u32[]{:S(2)}) copy-start(bf16[128,128]{1,0:T(8,128)(2,1)} %wo_ref.1) | copy-start | bytes 98308
  6.3 0.7 %copy-start.8 = (s32[2048]{0:T(1024)S(1)}, s32[2048]{0:T(1024)}, u32[]{:S(2)}) copy-start(s32[2048]{0:T(1024)} %param.26) | copy-start | bytes 24580

commit v2 on v1

v2 whole, which is shorter than its diff:
```python
import functools
import math

import jax
import jax.numpy as jnp
from jax import lax
from jax.experimental import pallas as pl
from jax.experimental.pallas import tpu as pltpu
from jax.sharding import PartitionSpec as P

H = 4
DH = 32
TILE = 128
HD = 128
COLS = 4
NB = 16
NSEL = 8
SLICE = 32
DEPTH = NSEL * TILE
LOG2E = math.log2(math.e)
MESH = pl.DeviceIdType.MESH
F32 = jnp.float32
BF16 = jnp.bfloat16

BIAS_IDS = ["A+1", "A-1", "A+2", "A-2", "A+3", "A-3", "A4", "B0", "B+1", "B-1", "B+2", "B-2", "B+3", "B-3", "B4"]
NORM_IDS = ["P+1", "P-1", "P2", "Q0", "Q+1", "Q-1", "Q2"]
SIB_IDS = ["P0"] + NORM_IDS
EARLY = ["A+0", "A+1", "A-1", "B0", "B+1", "B-1", "A+2", "A-2"]
LATE = ["B+2", "B-2", "A+3", "A-3", "A4", "B+3", "B-3", "B4"]


def nt(a, b):
    return lax.dot_general(a, b, (((1,), (1,)), ((), ())), preferred_element_type=F32)


def nn(a, b):
    return jnp.dot(a, b, preferred_element_type=F32)


def kernel(
    pair_in,
    gain_in,
    shift_in,
    wq_in,
    wk_in,
    wv_in,
    wg_in,
    gb_in,
    bias_ref,
    offset_in,
    chain_in,
    mask_in,
    out_ref,
    pair_ref,
    gain_ref,
    shift_ref,
    wq_ref,
    wk_ref,
    wv_ref,
    wg_ref,
    gb_ref,
    offset_ref,
    chain_ref,
    mask_ref,
    slices_ref,
    bias_all,
    norm_0,
    norm_1,
    rows_f32,
    qp_ref,
    gate_ref,
    chain_i_ref,
    s_ref,
    p_ref,
    o_ref,
    swap_send,
    swap_recv,
    bias_send,
    bias_recv,
    norm_send,
    norm_recv,
    sib_send,
    sib_recv,
    in_sem,
):
    r = lax.axis_index("row")
    c = lax.axis_index("col")
    core, yh, x = r % 2, (r // 2) % 2, r // 4
    z, yl = c % 8, c // 8
    norm_refs = (norm_0, norm_1)

    def row_of(dx, flip):
        return ((x + dx + 4) % 4) * 4 + ((yh + flip) % 2) * 2 + core

    def col_of(dz, flip):
        return ((yl + flip) % 2) * 8 + (z + dz + 8) % 8

    up = (r, col_of(1, 0))
    down = (r, col_of(-1, 0))
    across = (r, col_of(0, 1))
    right = (row_of(1, 0), c)
    left = (row_of(-1, 0), c)
    far = (row_of(0, 1), c)
    sib = (r + 1 - 2 * core, c)

    moves = [
        pltpu.make_async_copy(src, dst, in_sem.at[i])
        for i, (src, dst) in enumerate(
            (
                (pair_in, pair_ref),
                (gain_in, gain_ref),
                (shift_in, shift_ref),
                (wq_in, wq_ref),
                (wg_in, wg_ref),
                (gb_in, gb_ref),
                (wk_in, wk_ref),
                (mask_in, mask_ref),
                (offset_in, offset_ref),
                (chain_in, chain_ref),
                (wv_in, wv_ref),
                (bias_ref.at[pl.ds(c * SLICE, SLICE)], slices_ref.at[c]),
            )
        )
    ]
    for move in moves:
        move.start()

    swaps = [(flip * 8 + dz, (r, col_of(dz, flip))) for flip in range(2) for dz in range(8) if flip or dz]
    barrier = pltpu.get_barrier_semaphore()
    for peer in [peer for _, peer in swaps] + [right, left, far, sib]:
        pl.semaphore_signal(barrier, inc=1, device_id=peer, device_id_type=MESH)
    pl.semaphore_wait(barrier, 19)

    sends = []

    for index, peer in swaps:
        copy = pltpu.make_async_remote_copy(
            src_ref=bias_ref.at[pl.ds(peer[1] * SLICE, SLICE)],
            dst_ref=slices_ref.at[c],
            send_sem=swap_send.at[index],
            recv_sem=swap_recv.at[index],
            device_id=peer,
            device_id_type=MESH,
        )
        copy.start()
        sends.append(("w", copy))

    def wait_swaps():
        for index, _ in swaps:
            ref = slices_ref.at[col_of(-(index % 8), index // 8)]
            pltpu.make_async_remote_copy(
                src_ref=ref,
                dst_ref=ref,
                send_sem=swap_send.at[index],
                recv_sem=swap_recv.at[index],
                device_id=up,
                device_id_type=MESH,
            ).wait_recv()

    def bias_slot(name):
        return col_of(-int(name[1:]), 0 if name[0] == "A" else 1)

    def norm_slot(name):
        return row_of(-int(name[1:]), 0 if name[0] == "P" else 1)

    def send_bias(src_name, p, peer, as_name):
        ref = bias_all.at[bias_slot(src_name), pl.ds(p * 4, 4)]
        copy = pltpu.make_async_remote_copy(
            src_ref=ref,
            dst_ref=ref,
            send_sem=bias_send.at[len([s for s in sends if s[0] == "b"])],
            recv_sem=bias_recv.at[BIAS_IDS.index(as_name) * 2 + p],
            device_id=peer,
            device_id_type=MESH,
        )
        copy.start()
        sends.append(("b", copy))

    def wait_bias(name, p):
        ref = bias_all.at[bias_slot(name), pl.ds(p * 4, 4)]
        sem = bias_recv.at[BIAS_IDS.index(name) * 2 + p]
        pltpu.make_async_remote_copy(
            src_ref=ref, dst_ref=ref, send_sem=bias_send.at[0], recv_sem=sem, device_id=up, device_id_type=MESH
        ).wait_recv()

    def norm_part(name, p, e):
        ref = norm_refs[p].at[norm_slot(name)]
        return ref if e is None else ref.at[e]

    def norm_sem(name, p, e):
        return norm_recv.at[(NORM_IDS.index(name) * 2 + p) * 2 + (0 if e is None else e)]

    def send_norm(src_name, p, e, peer, as_name):
        ref = norm_part(src_name, p, e)
        copy = pltpu.make_async_remote_copy(
            src_ref=ref,
            dst_ref=ref,
            send_sem=norm_send.at[len([s for s in sends if s[0] == "n"])],
            recv_sem=norm_sem(as_name, p, e),
            device_id=peer,
            device_id_type=MESH,
        )
        copy.start()
        sends.append(("n", copy))

    def wait_norm(name, p, e=None):
        ref = norm_part(name, p, e)
        pltpu.make_async_remote_copy(
            src_ref=ref,
            dst_ref=ref,
            send_sem=norm_send.at[0],
            recv_sem=norm_sem(name, p, e),
            device_id=up,
            device_id_type=MESH,
        ).wait_recv()

    def send_sib(name, p):
        ref = norm_refs[p].at[norm_slot(name)]
        index = SIB_IDS.index(name) * 2 + p
        copy = pltpu.make_async_remote_copy(
            src_ref=ref,
            dst_ref=ref,
            send_sem=sib_send.at[index],
            recv_sem=sib_recv.at[index],
            device_id=sib,
            device_id_type=MESH,
        )
        copy.start()
        sends.append(("s", copy))

    def wait_sibs(p):
        for i, name in enumerate(SIB_IDS):
            ref = norm_refs[p].at[norm_slot(name) + 1 - 2 * core]
            pltpu.make_async_remote_copy(
                src_ref=ref,
                dst_ref=ref,
                send_sem=sib_send.at[i * 2 + p],
                recv_sem=sib_recv.at[i * 2 + p],
                device_id=sib,
                device_id_type=MESH,
            ).wait_recv()

    for move in moves[:3]:
        move.wait()
    values = pair_ref[...].astype(F32)
    center = values - jnp.mean(values, -1, keepdims=True)
    spread = jnp.mean(center * center, -1, keepdims=True)
    rows_f32[...] = center * lax.rsqrt(spread + 1e-05) * gain_ref[...] + shift_ref[...]
    for p in range(2):
        for e in range(2):
            norm_refs[p][r, e] = rows_f32[pl.ds(2 * p + e, TILE, stride=COLS), :].astype(BF16)
        send_norm("P0", p, None, right, "P+1")
        send_norm("P0", p, None, left, "P-1")
        send_norm("P0", p, None, far, "Q0")
        send_sib("P0", p)
    for move in moves[3:]:
        move.wait()

    picks = [jnp.int32(0) for _ in range(NSEL)]
    count = jnp.int32(0)
    for k in range(NB):
        flag = mask_ref[r, k]
        for n in range(NSEL):
            picks[n] = jnp.where((flag == 1) & (count == n), k, picks[n])
        count = count + jnp.where(flag == 1, 1, 0)
    pads = [jnp.where(n < count, 0.0, -1e30).astype(F32) for n in range(NSEL)]

    mine = jnp.concatenate([norm_refs[p][r].reshape(2 * TILE, HD) for p in range(2)], axis=0)
    query = (nn(mine, wq_ref[...]) * (1.0 / DH**0.5)).astype(BF16)
    head = lax.broadcasted_iota(jnp.int32, (TILE, HD), 1) // DH
    for j in range(COLS):
        part = query[j * TILE:(j + 1) * TILE]
        stacked = jnp.concatenate([jnp.where(head == h, part, jnp.zeros_like(part)) for h in range(H)], axis=0)
        qp_ref[j] = (nt(stacked, wk_ref[...]) * LOG2E).astype(BF16)

    wait_swaps()
    for n in range(NSEL):
        bias_all[c, n] = slices_ref[picks[n]]
    for p in range(2):
        send_bias("A0", p, up, "A+1")
        send_bias("A0", p, down, "A-1")
        send_bias("A0", p, across, "B0")

    gate_ref[...] = jax.nn.sigmoid(nn(mine, wg_ref[...]) + gb_ref[...])
    chain_i_ref[...] = jnp.transpose(jnp.broadcast_to(chain_ref[pl.ds(r, 1), :], (TILE, TILE)))

    for p in range(2):
        wait_norm("P+1", p)
        send_norm("P+1", p, 0, right, "P2")
        wait_norm("P-1", p)
        send_norm("P-1", p, 1, left, "P2")
        wait_norm("Q0", p)
        send_norm("Q0", p, None, right, "Q+1")
        send_norm("Q0", p, None, left, "Q-1")
        for name in ("P+1", "P-1", "Q0"):
            send_sib(name, p)
    for p in range(2):
        wait_bias("A+1", p)
        send_bias("A+1", p, up, "A+2")
        wait_bias("A-1", p)
        send_bias("A-1", p, down, "A-2")
        wait_bias("B0", p)
        send_bias("B0", p, up, "B+1")
        send_bias("B0", p, down, "B-1")
    for p in range(2):
        for name in ("Q+1", "Q-1"):
            wait_norm(name, p)
        send_norm("Q+1", p, 0, right, "Q2")
        send_norm("Q-1", p, 1, left, "Q2")
        wait_norm("P2", p, 0)
        wait_norm("P2", p, 1)
        for name in ("Q+1", "Q-1", "P2"):
            send_sib(name, p)
    for p in range(2):
        wait_bias("A+2", p)
        send_bias("A+2", p, up, "A+3")
        send_bias("A+2", p, across, "B+2")
        wait_bias("A-2", p)
        send_bias("A-2", p, down, "A-3")
        send_bias("A-2", p, across, "B-2")

    def keys_of(j, m):
        return jnp.concatenate([norm_refs[j // 2][picks[2 * m + e], j % 2] for e in range(2)], axis=0)

    def score(p):
        for j in range(2 * p, 2 * p + 2):
            queries = qp_ref[j]
            for m in range(NSEL // 2):
                s_ref[j, :, 2 * m * TILE:2 * (m + 1) * TILE] = nt(queries, keys_of(j, m))

    def finish_norm(p):
        wait_norm("Q2", p, 0)
        wait_norm("Q2", p, 1)
        send_sib("Q2", p)
        wait_sibs(p)

    finish_norm(0)
    score(0)
    for p in range(2):
        wait_bias("B+2", p)
        send_bias("B+2", p, up, "B+3")
        wait_bias("B-2", p)
        send_bias("B-2", p, down, "B-3")
        wait_bias("A+3", p)
        if p == 0:
            send_bias("A+3", p, up, "A4")
        wait_bias("A-3", p)
        if p == 1:
            send_bias("A-3", p, down, "A4")
    finish_norm(1)
    for p in range(2):
        wait_bias("A4", p)
        send_bias("A4", p, across, "B4")
    score(1)

    def softmax(batch, t, name):
        slot = bias_slot(name)
        rows = pl.ds(pl.multiple_of(slot * SLICE, SLICE), SLICE)
        chain_i = chain_i_ref[pl.ds(pl.multiple_of((slot % 4) * SLICE, SLICE), SLICE), :]
        extra = offset_ref[slot // 4]
        parts = []
        for n in range(NSEL):
            differs = chain_i != chain_ref[pl.ds(picks[n], 1), :]
            parts.append((bias_all[slot, n].astype(F32) + jnp.where(differs, extra, 0.0) + pads[n]) * LOG2E)
        bias = jnp.concatenate(parts, axis=1)
        inverse = []
        for j in range(COLS):
            scores = s_ref[j, rows, :] + bias
            expo = jnp.exp2(scores - jnp.max(scores, axis=-1, keepdims=True))
            inverse.append(1.0 / jnp.sum(expo, axis=-1, keepdims=True))
            p_ref[batch, j, t * SLICE:(t + 1) * SLICE, :] = expo.astype(BF16)
        return rows, inverse

    def mix(batch, done):
        for j in range(COLS):
            keys = jnp.concatenate([keys_of(j, m) for m in range(NSEL // 2)], axis=0)
            summed = nn(p_ref[batch, j], keys)
            for t, (rows, inverse) in enumerate(done):
                o_ref[j, rows, :] = summed[t * SLICE:(t + 1) * SLICE] * inverse[j]

    for name in ("B+1", "B-1"):
        for p in range(2):
            wait_bias(name, p)
    done = [softmax(0, t, name) for t, name in enumerate(EARLY)]
    mix(0, done)
    for name in ("B+3", "B-3", "B4"):
        for p in range(2):
            wait_bias(name, p)
    done = [softmax(1, t, name) for t, name in enumerate(LATE)]
    mix(1, done)

    for j in range(COLS):
        mixed = o_ref[j]
        high = mixed.astype(BF16)
        low = (mixed - high.astype(F32)).astype(BF16)
        heads = nn(high, wv_ref[...]) + nn(low, wv_ref[...])
        attended = jnp.where(head == 0, heads[:TILE], 0.0)
        for h in range(1, H):
            attended = jnp.where(head == h, heads[h * TILE:(h + 1) * TILE], attended)
        rows_f32[pl.ds(j, TILE, stride=COLS), :] = gate_ref[j * TILE:(j + 1) * TILE, :] * attended
    out_ref[...] = rows_f32[...].astype(BF16)

    for _, copy in sends:
        copy.wait_send()


def on_device(
    pair,
    norm_gain,
    norm_offset,
    w_query,
    w_key,
    w_value,
    w_gate,
    gate_bias,
    w_out,
    out_bias,
    bias,
    chain_offset,
    chain_ids,
    tile_mask,
):
    hbm = pl.BlockSpec(memory_space=pltpu.HBM)
    vector = pltpu.VMEM((1, HD), F32)
    matrix = pltpu.VMEM((HD, HD), BF16)
    gated = pl.pallas_call(
        kernel,
        out_shape=jax.ShapeDtypeStruct((TILE * COLS, HD), BF16),
        in_specs=[hbm] * 12,
        out_specs=pl.BlockSpec(memory_space=pltpu.VMEM),
        scratch_shapes=[
            pltpu.VMEM((TILE * COLS, HD), BF16),
            vector,
            vector,
            matrix,
            matrix,
            matrix,
            matrix,
            vector,
            pltpu.SMEM((H,), F32),
            pltpu.VMEM((NB, TILE), jnp.int32),
            pltpu.SMEM((NB, NB), jnp.int32),
            pltpu.VMEM((NB, SLICE, TILE), BF16),
            pltpu.VMEM((NB, NSEL, SLICE, TILE), BF16),
            pltpu.VMEM((NB, 2, TILE, HD), BF16),
            pltpu.VMEM((NB, 2, TILE, HD), BF16),
            pltpu.VMEM((TILE * COLS, HD), F32),
            pltpu.VMEM((COLS, H * TILE, HD), BF16),
            pltpu.VMEM((COLS * TILE, HD), F32),
            pltpu.VMEM((TILE, TILE), jnp.int32),
            pltpu.VMEM((COLS, H * TILE, DEPTH), F32),
            pltpu.VMEM((2, COLS, 8 * SLICE, DEPTH), BF16),
            pltpu.VMEM((COLS, H * TILE, HD), F32),
            pltpu.SemaphoreType.DMA((16,)),
            pltpu.SemaphoreType.DMA((16,)),
            pltpu.SemaphoreType.DMA((32,)),
            pltpu.SemaphoreType.DMA((30,)),
            pltpu.SemaphoreType.DMA((20,)),
            pltpu.SemaphoreType.DMA((28,)),
            pltpu.SemaphoreType.DMA((16,)),
            pltpu.SemaphoreType.DMA((16,)),
            pltpu.SemaphoreType.DMA((12,)),
        ],
        compiler_params=pltpu.CompilerParams(
            collective_id=0, has_side_effects=True, vmem_limit_bytes=64 * 1024 * 1024
        ),
        cost_estimate=pl.CostEstimate(flops=1 << 30, bytes_accessed=1 << 20, transcendentals=1 << 21),
    )(
        pair.reshape(TILE * COLS, HD),
        norm_gain.reshape(1, HD),
        norm_offset.reshape(1, HD),
        w_query,
        w_key,
        w_value,
        w_gate,
        gate_bias.reshape(1, HD),
        bias.reshape(H * TILE, TILE),
        chain_offset,
        chain_ids.reshape(NB, TILE),
        tile_mask,
    )
    update = jnp.dot(gated, w_out, preferred_element_type=F32) + out_bias
    return update.astype(BF16).reshape(TILE, COLS, HD)


def solution(mesh):
    placed = (
        P("row", "col", None),
        P(),
        P(),
        P(),
        P(),
        P(),
        P(),
        P(),
        P(),
        P(),
        P(None, "row", "col"),
        P(),
        P(),
        P(),
    )
    return jax.shard_map(
        on_device, mesh=mesh, in_specs=placed, out_specs=P("row", "col", None), check_vma=False
    )
```

time: 45.8 us -> 39.1 us (0.85)
  the two profiles are of different devices: /device:TPU:2 before, /device:TPU:1 now
where the time goes in v2:
time: 39.1 us; the launch traced here: 39 us
  Pallas kernels  37.2 us (95%)
  matrix products  1.76 us (5%)
    pallas_call x1, Pallas kernels, on_device(): pl.pallas_call(kernel, out_shape=jax.ShapeDtypeStruct((TILE * COLS, HD),...  37.2 us
    dot_general x1, matrix products, on_device(): update = jnp.dot(gated, w_out, preferred_element_type=F32) + out_bias  1.76 us

profile of v2, /device:TPU:1, one launch (start us, length us, event | category | flops | bytes accessed | tf_op | source)
XLA Modules:
  0.0 39.0 jit_solution(9544367875653673952)
XLA Ops:
  0.0 37.2 %shard_map.136 = bf16[512,128]{1,0:T(8,128)(2,1)} custom-call(bf16[512,128]{1,0:T(8,128)(2,1)} %bitcast.9, f32[1,128]{1,0:T(1,128)} %bitcast.12, f32[1,128]{1,0:T(1,128)} %bitcast.13, bf16[128,128]{1,0:T(8,128)(2,1)} %wq_in.1, bf16[128,128]{1,0:T(8,128)(2,1)} %wk_in.1, bf16[128,128]{1,0:T(8,128)(2,1)} %wv_in.1, bf16[128,128]{1,0:T(8,128)(2,1)} %wg_in.1, ...), custom_call_target="tpu_custom_call" | custom-call | flops 1073741824 | bytes 1048576 | tf_op jit(solution)/shard_map/pallas_call | solution.py:426
  37.3 1.8 %fusion = bf16[512,128]{1,0:T(8,128)(2,1)} fusion(bf16[512,128]{1,0:T(8,128)(2,1)} %shard_map.136, bf16[128,128]{1,0:T(8,128)(2,1)} %param.22, f32[128]{0:T(128)} %param.23), kind=kOutput, calls=%fused_computation.1 | convolution fusion | flops 16908288 | bytes 295424 | tf_op jit(solution)/shard_map/dot_general | solution.py:482

commit v3 on v2

--- a/solution.py
+++ b/solution.py
@@ -70,6 +70,7 @@
     qp_ref,
     gate_ref,
     chain_i_ref,
+    bx_ref,
     s_ref,
     p_ref,
     o_ref,
@@ -101,6 +102,9 @@
     right = (row_of(1, 0), c)
     left = (row_of(-1, 0), c)
     far = (row_of(0, 1), c)
+    up2 = (r, col_of(2, 0))
+    down2 = (r, col_of(-2, 0))
+    opposite = (row_of(2, 0), c)
     sib = (r + 1 - 2 * core, c)
 
     moves = [
@@ -125,25 +129,12 @@
     for move in moves:
         move.start()
 
-    swaps = [(flip * 8 + dz, (r, col_of(dz, flip))) for flip in range(2) for dz in range(8) if flip or dz]
+    swaps = [(flip * 8 + dz, (r, col_of(dz, flip))) for dz in (4, 3, 5, 2, 6, 1, 7, 0) for flip in (1, 0) if flip or dz]
     barrier = pltpu.get_barrier_semaphore()
-    for peer in [peer for _, peer in swaps] + [right, left, far, sib]:
+    for peer in [peer for _, peer in swaps] + [right, left, far, sib, opposite]:
         pl.semaphore_signal(barrier, inc=1, device_id=peer, device_id_type=MESH)
-    pl.semaphore_wait(barrier, 19)
 
     sends = []
-
-    for index, peer in swaps:
-        copy = pltpu.make_async_remote_copy(
-            src_ref=bias_ref.at[pl.ds(peer[1] * SLICE, SLICE)],
-            dst_ref=slices_ref.at[c],
-            send_sem=swap_send.at[index],
-            recv_sem=swap_recv.at[index],
-            device_id=peer,
-            device_id_type=MESH,
-        )
-        copy.start()
-        sends.append(("w", copy))
 
     def wait_swaps():
         for index, _ in swaps:
@@ -228,17 +219,17 @@
         copy.start()
         sends.append(("s", copy))
 
-    def wait_sibs(p):
-        for i, name in enumerate(SIB_IDS):
-            ref = norm_refs[p].at[norm_slot(name) + 1 - 2 * core]
-            pltpu.make_async_remote_copy(
-                src_ref=ref,
-                dst_ref=ref,
-                send_sem=sib_send.at[i * 2 + p],
-                recv_sem=sib_recv.at[i * 2 + p],
-                device_id=sib,
-                device_id_type=MESH,
-            ).wait_recv()
+    def wait_sib(name, p):
+        ref = norm_refs[p].at[norm_slot(name) + 1 - 2 * core]
+        index = SIB_IDS.index(name) * 2 + p
+        pltpu.make_async_remote_copy(
+            src_ref=ref,
+            dst_ref=ref,
+            send_sem=sib_send.at[index],
+            recv_sem=sib_recv.at[index],
+            device_id=sib,
+            device_id_type=MESH,
+        ).wait_recv()
 
     for move in moves[:3]:
         move.wait()
@@ -249,9 +240,26 @@
     for p in range(2):
         for e in range(2):
             norm_refs[p][r, e] = rows_f32[pl.ds(2 * p + e, TILE, stride=COLS), :].astype(BF16)
+
+    pl.semaphore_wait(barrier, 20)
+    for p in range(2):
+        send_norm("P0", p, None, far, "Q0")
         send_norm("P0", p, None, right, "P+1")
         send_norm("P0", p, None, left, "P-1")
-        send_norm("P0", p, None, far, "Q0")
+
+    for index, peer in swaps:
+        copy = pltpu.make_async_remote_copy(
+            src_ref=bias_ref.at[pl.ds(peer[1] * SLICE, SLICE)],
+            dst_ref=slices_ref.at[c],
+            send_sem=swap_send.at[index],
+            recv_sem=swap_recv.at[index],
+            device_id=peer,
+            device_id_type=MESH,
+        )
+        copy.start()
+        sends.append(("w", copy))
+
+    for p in range(2):
         send_sib("P0", p)
     for move in moves[3:]:
         move.wait()
@@ -273,121 +281,133 @@
         stacked = jnp.concatenate([jnp.where(head == h, part, jnp.zeros_like(part)) for h in range(H)], axis=0)
         qp_ref[j] = (nt(stacked, wk_ref[...]) * LOG2E).astype(BF16)
 
-    wait_swaps()
-    for n in range(NSEL):
-        bias_all[c, n] = slices_ref[picks[n]]
-    for p in range(2):
-        send_bias("A0", p, up, "A+1")
-        send_bias("A0", p, down, "A-1")
-        send_bias("A0", p, across, "B0")
-
     gate_ref[...] = jax.nn.sigmoid(nn(mine, wg_ref[...]) + gb_ref[...])
     chain_i_ref[...] = jnp.transpose(jnp.broadcast_to(chain_ref[pl.ds(r, 1), :], (TILE, TILE)))
 
-    for p in range(2):
+    def keys_of(j, m):
+        return jnp.concatenate([norm_refs[j // 2][picks[2 * m + e], j % 2] for e in range(2)], axis=0)
+
+    def score(name, p):
+        wait_sib(name, p)
+        first = norm_slot(name) - core
+        for e in range(2):
+            keys = norm_refs[p][pl.ds(first, 2), e].reshape(2 * TILE, HD)
+            both = nt(qp_ref[2 * p + e], keys)
+            s_ref[2 * p + e, first] = both[:, :TILE]
+            s_ref[2 * p + e, first + 1] = both[:, TILE:]
+
+    def pass_first(p):
+        wait_norm("Q0", p)
+        send_norm("Q0", p, None, right, "Q+1")
+        send_norm("Q0", p, None, left, "Q-1")
+        send_norm("Q0", p, None, opposite, "Q2")
         wait_norm("P+1", p)
         send_norm("P+1", p, 0, right, "P2")
         wait_norm("P-1", p)
         send_norm("P-1", p, 1, left, "P2")
-        wait_norm("Q0", p)
-        send_norm("Q0", p, None, right, "Q+1")
-        send_norm("Q0", p, None, left, "Q-1")
         for name in ("P+1", "P-1", "Q0"):
             send_sib(name, p)
-    for p in range(2):
-        wait_bias("A+1", p)
-        send_bias("A+1", p, up, "A+2")
-        wait_bias("A-1", p)
-        send_bias("A-1", p, down, "A-2")
-        wait_bias("B0", p)
-        send_bias("B0", p, up, "B+1")
-        send_bias("B0", p, down, "B-1")
-    for p in range(2):
+
+    def pass_second(p):
+        wait_norm("P2", p, 0)
+        wait_norm("P2", p, 1)
         for name in ("Q+1", "Q-1"):
             wait_norm(name, p)
-        send_norm("Q+1", p, 0, right, "Q2")
-        send_norm("Q-1", p, 1, left, "Q2")
-        wait_norm("P2", p, 0)
-        wait_norm("P2", p, 1)
-        for name in ("Q+1", "Q-1", "P2"):
+        for name in ("P2", "Q+1", "Q-1"):
             send_sib(name, p)
+
+    for p in range(2):
+        score("P0", p)
+    pass_first(0)
+    wait_swaps()
+    for n in range(NSEL):
+        bias_all[c, n] = slices_ref[picks[n]]
+    for p in range(2):
+        send_bias("A0", p, up, "A+1")
+        send_bias("A0", p, down, "A-1")
+        send_bias("A0", p, across, "B0")
+    for p in range(2):
+        send_bias("A0", p, up2, "A+2")
+        send_bias("A0", p, down2, "A-2")
+    pass_first(1)
+    for name in ("P+1", "P-1", "Q0"):
+        score(name, 0)
+    for p in range(2):
+        wait_bias("A+1", p)
+        send_bias("A+1", p, across, "B+1")
+        wait_bias("A-1", p)
+        send_bias("A-1", p, across, "B-1")
+    for name in ("P+1", "P-1", "Q0"):
+        score(name, 1)
+    pass_second(0)
     for p in range(2):
         wait_bias("A+2", p)
+        if p == 0:
+            send_bias("A+2", p, up2, "A4")
+        send_bias("A+2", p, across, "B+2")
         send_bias("A+2", p, up, "A+3")
-        send_bias("A+2", p, across, "B+2")
         wait_bias("A-2", p)
+        if p == 1:
+            send_bias("A-2", p, down2, "A4")
+        send_bias("A-2", p, across, "B-2")
         send_bias("A-2", p, down, "A-3")
-        send_bias("A-2", p, across, "B-2")
-
-    def keys_of(j, m):
-        return jnp.concatenate([norm_refs[j // 2][picks[2 * m + e], j % 2] for e in range(2)], axis=0)
-
-    def score(p):
-        for j in range(2 * p, 2 * p + 2):
-            queries = qp_ref[j]
-            for m in range(NSEL // 2):
-                s_ref[j, :, 2 * m * TILE:2 * (m + 1) * TILE] = nt(queries, keys_of(j, m))
-
-    def finish_norm(p):
-        wait_norm("Q2", p, 0)
-        wait_norm("Q2", p, 1)
-        send_sib("Q2", p)
-        wait_sibs(p)
-
-    finish_norm(0)
-    score(0)
+    for name in ("P2", "Q+1", "Q-1"):
+        score(name, 0)
+    pass_second(1)
+    wait_norm("Q2", 0)
+    send_sib("Q2", 0)
     for p in range(2):
         wait_bias("B+2", p)
         send_bias("B+2", p, up, "B+3")
         wait_bias("B-2", p)
         send_bias("B-2", p, down, "B-3")
-        wait_bias("A+3", p)
-        if p == 0:
-            send_bias("A+3", p, up, "A4")
-        wait_bias("A-3", p)
-        if p == 1:
-            send_bias("A-3", p, down, "A4")
-    finish_norm(1)
-    for p in range(2):
         wait_bias("A4", p)
         send_bias("A4", p, across, "B4")
-    score(1)
-
-    def softmax(batch, t, name):
+    wait_norm("Q2", 1)
+    send_sib("Q2", 1)
+    for name in ("P2", "Q+1", "Q-1"):
+        score(name, 1)
+
+    def prepare(batch, t, name):
         slot = bias_slot(name)
-        rows = pl.ds(pl.multiple_of(slot * SLICE, SLICE), SLICE)
         chain_i = chain_i_ref[pl.ds(pl.multiple_of((slot % 4) * SLICE, SLICE), SLICE), :]
         extra = offset_ref[slot // 4]
-        parts = []
         for n in range(NSEL):
             differs = chain_i != chain_ref[pl.ds(picks[n], 1), :]
-            parts.append((bias_all[slot, n].astype(F32) + jnp.where(differs, extra, 0.0) + pads[n]) * LOG2E)
-        bias = jnp.concatenate(parts, axis=1)
-        inverse = []
-        for j in range(COLS):
-            scores = s_ref[j, rows, :] + bias
-            expo = jnp.exp2(scores - jnp.max(scores, axis=-1, keepdims=True))
-            inverse.append(1.0 / jnp.sum(expo, axis=-1, keepdims=True))
-            p_ref[batch, j, t * SLICE:(t + 1) * SLICE, :] = expo.astype(BF16)
-        return rows, inverse
-
-    def mix(batch, done):
-        for j in range(COLS):
+            part = (bias_all[slot, n].astype(F32) + jnp.where(differs, extra, 0.0) + pads[n]) * LOG2E
+            bx_ref[batch, t * SLICE:(t + 1) * SLICE, n * TILE:(n + 1) * TILE] = part
+
+    def attend(batch, names, p):
+        rows = [pl.ds(pl.multiple_of(bias_slot(name) * SLICE, SLICE), SLICE) for name in names]
+        for j in range(2 * p, 2 * p + 2):
+            inverse = []
+            for t in range(len(names)):
+                block = slice(t * SLICE, (t + 1) * SLICE)
+                scores = jnp.concatenate([s_ref[j, picks[n], rows[t], :] for n in range(NSEL)], axis=1)
+                scores = scores + bx_ref[batch, block, :]
+                expo = jnp.exp2(scores - jnp.max(scores, axis=-1, keepdims=True))
+                inverse.append(1.0 / jnp.sum(expo, axis=-1, keepdims=True))
+                p_ref[batch, j, block, :] = expo.astype(BF16)
             keys = jnp.concatenate([keys_of(j, m) for m in range(NSEL // 2)], axis=0)
             summed = nn(p_ref[batch, j], keys)
-            for t, (rows, inverse) in enumerate(done):
-                o_ref[j, rows, :] = summed[t * SLICE:(t + 1) * SLICE] * inverse[j]
-
-    for name in ("B+1", "B-1"):
+            for t in range(len(names)):
+                o_ref[j, rows[t], :] = summed[t * SLICE:(t + 1) * SLICE] * inverse[t]
+
+    for name in ("B0", "B+1", "B-1"):
         for p in range(2):
             wait_bias(name, p)
-    done = [softmax(0, t, name) for t, name in enumerate(EARLY)]
-    mix(0, done)
-    for name in ("B+3", "B-3", "B4"):
+    for t, name in enumerate(EARLY):
+        prepare(0, t, name)
+    for p in range(2):
+        score("Q2", p)
+        attend(0, EARLY, p)
+    for name in ("A+3", "A-3", "B+3", "B-3", "B4"):
         for p in range(2):
             wait_bias(name, p)
-    done = [softmax(1, t, name) for t, name in enumerate(LATE)]
-    mix(1, done)
+    for t, name in enumerate(LATE):
+        prepare(1, t, name)
+    for p in range(2):
+        attend(1, LATE, p)
 
     for j in range(COLS):
         mixed = o_ref[j]
@@ -448,7 +468,8 @@
             pltpu.VMEM((COLS, H * TILE, HD), BF16),
             pltpu.VMEM((COLS * TILE, HD), F32),
             pltpu.VMEM((TILE, TILE), jnp.int32),
-            pltpu.VMEM((COLS, H * TILE, DEPTH), F32),
+            pltpu.VMEM((2, 8 * SLICE, DEPTH), F32),
+            pltpu.VMEM((COLS, NB, H * TILE, TILE), F32),
             pltpu.VMEM((2, COLS, 8 * SLICE, DEPTH), BF16),
             pltpu.VMEM((COLS, H * TILE, HD), F32),
             pltpu.SemaphoreType.DMA((16,)),

time: 39.1 us -> 35.5 us (0.908)
  Pallas kernels: 37.2 us -> 33.7 us
    pallas_call x1, Pallas kernels: 37.2 us -> 33.7 us  [on_device(): pl.pallas_call(kernel, out_shape=jax.ShapeDtypeStruct((TILE * COLS, HD),...]
where the time goes in v3:
time: 35.5 us; the launch traced here: 35.4 us
  Pallas kernels  33.7 us (95%)
  matrix products  1.75 us (5%)
    pallas_call x1, Pallas kernels, on_device(): pl.pallas_call(kernel, out_shape=jax.ShapeDtypeStruct((TILE * COLS, HD),...  33.7 us
    dot_general x1, matrix products, on_device(): update = jnp.dot(gated, w_out, preferred_element_type=F32) + out_bias  1.75 us

profile of v3, /device:TPU:1, one launch (start us, length us, event | category | flops | bytes accessed | tf_op | source)
XLA Modules:
  0.0 35.4 jit_solution(12851260562168571377)
XLA Ops:
  0.0 33.7 %shard_map.136 = bf16[512,128]{1,0:T(8,128)(2,1)} custom-call(bf16[512,128]{1,0:T(8,128)(2,1)} %bitcast.9, f32[1,128]{1,0:T(1,128)} %bitcast.12, f32[1,128]{1,0:T(1,128)} %bitcast.13, bf16[128,128]{1,0:T(8,128)(2,1)} %wq_in.1, bf16[128,128]{1,0:T(8,128)(2,1)} %wk_in.1, bf16[128,128]{1,0:T(8,128)(2,1)} %wv_in.1, bf16[128,128]{1,0:T(8,128)(2,1)} %wg_in.1, ...), custom_call_target="tpu_custom_call" | custom-call | flops 1073741824 | bytes 1048576 | tf_op jit(solution)/shard_map/pallas_call | solution.py:446
  33.7 1.8 %fusion = bf16[512,128]{1,0:T(8,128)(2,1)} fusion(bf16[512,128]{1,0:T(8,128)(2,1)} %shard_map.136, bf16[128,128]{1,0:T(8,128)(2,1)} %param.22, f32[128]{0:T(128)} %param.23), kind=kOutput, calls=%fused_computation.1 | convolution fusion | flops 16908288 | bytes 295424 | tf_op jit(solution)/shard_map/dot_general | solution.py:503

commit v4 on v3

--- a/solution.py
+++ b/solution.py
@@ -298,9 +298,9 @@
 
     def pass_first(p):
         wait_norm("Q0", p)
+        send_norm("Q0", p, None, opposite, "Q2")
         send_norm("Q0", p, None, right, "Q+1")
         send_norm("Q0", p, None, left, "Q-1")
-        send_norm("Q0", p, None, opposite, "Q2")
         wait_norm("P+1", p)
         send_norm("P+1", p, 0, right, "P2")
         wait_norm("P-1", p)
@@ -333,13 +333,11 @@
     for name in ("P+1", "P-1", "Q0"):
         score(name, 0)
     for p in range(2):
-        wait_bias("A+1", p)
-        send_bias("A+1", p, across, "B+1")
-        wait_bias("A-1", p)
-        send_bias("A-1", p, across, "B-1")
+        wait_bias("B0", p)
+        send_bias("B0", p, up, "B+1")
+        send_bias("B0", p, down, "B-1")
     for name in ("P+1", "P-1", "Q0"):
         score(name, 1)
-    pass_second(0)
     for p in range(2):
         wait_bias("A+2", p)
         if p == 0:
@@ -351,11 +349,12 @@
             send_bias("A-2", p, down2, "A4")
         send_bias("A-2", p, across, "B-2")
         send_bias("A-2", p, down, "A-3")
+    pass_second(0)
+    wait_norm("Q2", 0)
+    send_sib("Q2", 0)
     for name in ("P2", "Q+1", "Q-1"):
         score(name, 0)
     pass_second(1)
-    wait_norm("Q2", 0)
-    send_sib("Q2", 0)
     for p in range(2):
         wait_bias("B+2", p)
         send_bias("B+2", p, up, "B+3")
@@ -365,8 +364,7 @@
         send_bias("A4", p, across, "B4")
     wait_norm("Q2", 1)
     send_sib("Q2", 1)
-    for name in ("P2", "Q+1", "Q-1"):
-        score(name, 1)
+    score("Q2", 0)
 
     def prepare(batch, t, name):
         slot = bias_slot(name)
@@ -393,14 +391,15 @@
             for t in range(len(names)):
                 o_ref[j, rows[t], :] = summed[t * SLICE:(t + 1) * SLICE] * inverse[t]
 
-    for name in ("B0", "B+1", "B-1"):
+    for name in ("A+1", "A-1", "B+1", "B-1"):
         for p in range(2):
             wait_bias(name, p)
     for t, name in enumerate(EARLY):
         prepare(0, t, name)
-    for p in range(2):
-        score("Q2", p)
-        attend(0, EARLY, p)
+    attend(0, EARLY, 0)
+    for name in ("P2", "Q+1", "Q-1", "Q2"):
+        score(name, 1)
+    attend(0, EARLY, 1)
     for name in ("A+3", "A-3", "B+3", "B-3", "B4"):
         for p in range(2):
             wait_bias(name, p)

time: 35.5 us -> 34.6 us (0.975)
  Pallas kernels: 33.7 us -> 32.7 us
    pallas_call x1, Pallas kernels: 33.7 us -> 32.7 us  [on_device(): pl.pallas_call(kernel, out_shape=jax.ShapeDtypeStruct((TILE * COLS, HD),...]
where the time goes in v4:
time: 34.6 us; the launch traced here: 34.5 us
  Pallas kernels  32.7 us (95%)
  matrix products  1.76 us (5%)
    pallas_call x1, Pallas kernels, on_device(): pl.pallas_call(kernel, out_shape=jax.ShapeDtypeStruct((TILE * COLS, HD),...  32.7 us
    dot_general x1, matrix products, on_device(): update = jnp.dot(gated, w_out, preferred_element_type=F32) + out_bias  1.76 us

profile of v4, /device:TPU:1, one launch (start us, length us, event | category | flops | bytes accessed | tf_op | source)
XLA Modules:
  0.0 34.5 jit_solution(12073513266140967791)
XLA Ops:
  0.0 32.7 %shard_map.136 = bf16[512,128]{1,0:T(8,128)(2,1)} custom-call(bf16[512,128]{1,0:T(8,128)(2,1)} %bitcast.9, f32[1,128]{1,0:T(1,128)} %bitcast.12, f32[1,128]{1,0:T(1,128)} %bitcast.13, bf16[128,128]{1,0:T(8,128)(2,1)} %wq_in.1, bf16[128,128]{1,0:T(8,128)(2,1)} %wk_in.1, bf16[128,128]{1,0:T(8,128)(2,1)} %wv_in.1, bf16[128,128]{1,0:T(8,128)(2,1)} %wg_in.1, ...), custom_call_target="tpu_custom_call" | custom-call | flops 1073741824 | bytes 1048576 | tf_op jit(solution)/shard_map/pallas_call | solution.py:445
  32.7 1.8 %fusion = bf16[512,128]{1,0:T(8,128)(2,1)} fusion(bf16[512,128]{1,0:T(8,128)(2,1)} %shard_map.136, bf16[128,128]{1,0:T(8,128)(2,1)} %param.22, f32[128]{0:T(128)} %param.23), kind=kOutput, calls=%fused_computation.1 | convolution fusion | flops 16908288 | bytes 295424 | tf_op jit(solution)/shard_map/dot_general | solution.py:502

commit v5 on v4

--- a/solution.py
+++ b/solution.py
@@ -273,17 +273,6 @@
         count = count + jnp.where(flag == 1, 1, 0)
     pads = [jnp.where(n < count, 0.0, -1e30).astype(F32) for n in range(NSEL)]
 
-    mine = jnp.concatenate([norm_refs[p][r].reshape(2 * TILE, HD) for p in range(2)], axis=0)
-    query = (nn(mine, wq_ref[...]) * (1.0 / DH**0.5)).astype(BF16)
-    head = lax.broadcasted_iota(jnp.int32, (TILE, HD), 1) // DH
-    for j in range(COLS):
-        part = query[j * TILE:(j + 1) * TILE]
-        stacked = jnp.concatenate([jnp.where(head == h, part, jnp.zeros_like(part)) for h in range(H)], axis=0)
-        qp_ref[j] = (nt(stacked, wk_ref[...]) * LOG2E).astype(BF16)
-
-    gate_ref[...] = jax.nn.sigmoid(nn(mine, wg_ref[...]) + gb_ref[...])
-    chain_i_ref[...] = jnp.transpose(jnp.broadcast_to(chain_ref[pl.ds(r, 1), :], (TILE, TILE)))
-
     def keys_of(j, m):
         return jnp.concatenate([norm_refs[j // 2][picks[2 * m + e], j % 2] for e in range(2)], axis=0)
 
@@ -316,8 +305,6 @@
         for name in ("P2", "Q+1", "Q-1"):
             send_sib(name, p)
 
-    for p in range(2):
-        score("P0", p)
     pass_first(0)
     wait_swaps()
     for n in range(NSEL):
@@ -329,7 +316,20 @@
     for p in range(2):
         send_bias("A0", p, up2, "A+2")
         send_bias("A0", p, down2, "A-2")
+    mine = jnp.concatenate([norm_refs[p][r].reshape(2 * TILE, HD) for p in range(2)], axis=0)
+    query = (nn(mine, wq_ref[...]) * (1.0 / DH**0.5)).astype(BF16)
+    head = lax.broadcasted_iota(jnp.int32, (TILE, HD), 1) // DH
+    for j in range(COLS):
+        part = query[j * TILE:(j + 1) * TILE]
+        stacked = jnp.concatenate([jnp.where(head == h, part, jnp.zeros_like(part)) for h in range(H)], axis=0)
+        qp_ref[j] = (nt(stacked, wk_ref[...]) * LOG2E).astype(BF16)
+
+    gate_ref[...] = jax.nn.sigmoid(nn(mine, wg_ref[...]) + gb_ref[...])
+    chain_i_ref[...] = jnp.transpose(jnp.broadcast_to(chain_ref[pl.ds(r, 1), :], (TILE, TILE)))
+
     pass_first(1)
+    for p in range(2):
+        score("P0", p)
     for name in ("P+1", "P-1", "Q0"):
         score(name, 0)
     for p in range(2):

time: 34.6 us -> 34.6 us (level)
  no operation moved by 1% of the time
where the time goes in v5:
time: 34.6 us; the launch traced here: 34.5 us
  Pallas kernels  32.7 us (95%)
  matrix products  1.76 us (5%)
    pallas_call x1, Pallas kernels, on_device(): pl.pallas_call(kernel, out_shape=jax.ShapeDtypeStruct((TILE * COLS, HD),...  32.7 us
    dot_general x1, matrix products, on_device(): update = jnp.dot(gated, w_out, preferred_element_type=F32) + out_bias  1.76 us

profile of v5, /device:TPU:1, one launch (start us, length us, event | category | flops | bytes accessed | tf_op | source)
XLA Modules:
  0.0 34.5 jit_solution(15640108114717334334)
XLA Ops:
  0.0 32.7 %shard_map.136 = bf16[512,128]{1,0:T(8,128)(2,1)} custom-call(bf16[512,128]{1,0:T(8,128)(2,1)} %bitcast.9, f32[1,128]{1,0:T(1,128)} %bitcast.12, f32[1,128]{1,0:T(1,128)} %bitcast.13, bf16[128,128]{1,0:T(8,128)(2,1)} %wq_in.1, bf16[128,128]{1,0:T(8,128)(2,1)} %wk_in.1, bf16[128,128]{1,0:T(8,128)(2,1)} %wv_in.1, bf16[128,128]{1,0:T(8,128)(2,1)} %wg_in.1, ...), custom_call_target="tpu_custom_call" | custom-call | flops 1073741824 | bytes 1048576 | tf_op jit(solution)/shard_map/pallas_call | solution.py:445
  32.7 1.8 %fusion = bf16[512,128]{1,0:T(8,128)(2,1)} fusion(bf16[512,128]{1,0:T(8,128)(2,1)} %shard_map.136, bf16[128,128]{1,0:T(8,128)(2,1)} %param.22, f32[128]{0:T(128)} %param.23), kind=kOutput, calls=%fused_computation.1 | convolution fusion | flops 16908288 | bytes 295424 | tf_op jit(solution)/shard_map/dot_general | solution.py:502
